TPU v7x, 512 devices: a whole 4x4x16 slice. The times are simulated.
512 devices in a mesh: space: 64 (over y, z), dp: 8 (over x, core).
Axes of the slice: x: 4, y: 4, z: 16, core: 2. Of those that a mesh axis runs over, the one named last changes fastest.
Arguments:
- coarse_latents: bfloat16 [8, 4096, 512], P('dp', 'space'), may hold values from -6 to 6
- active_blocks: int32 [8, 128], P('dp'), may hold values from 0 to 4095, as said below
- face_links: int32 [8, 128, 6], P('dp', 'space'), may hold values from -1 to 127, as said below
- cotangent: bfloat16 [8, 128, 8, 8, 256], P('dp', 'space'), may hold values from -6 to 6
- up_weight: bfloat16 [64, 2048], replicated, may hold values from -0.75 to 0.75
- conv_one: bfloat16 [27, 32, 32], replicated, may hold values from -0.21875 to 0.21875
- conv_two: bfloat16 [27, 32, 32], replicated, may hold values from -0.21875 to 0.21875
Outputs:
- fine: bfloat16 [8, 128, 8, 8, 256], P('dp', 'space')
- grad_one: float32 [27, 32, 32], replicated
- grad_two: float32 [27, 32, 32], replicated
Inputs may be any that keep to these rules, and one draw needn't show every extreme that they name: `active_blocks`: call the bricks at positions i * 2 to (i + 1) * 2 - 1 group i and the block rows i * 64 to (i + 1) * 64 - 1 range i. At most 2 bricks of one group take their blocks from one range, and in every scene every group has exactly 2 from some range. `face_links`: links are mutual: if brick h is the neighbour of g across face f, g is the neighbour of h across the opposite face. A neighbour of brick g lies at a position whose quotient by 2 differs from that of g by at most one; across a -x, -y or -z face that quotient is never larger than that of g, across a +x, +y or +z face never smaller.
All inputs are finite; a program needn't handle non-finite values.
Results may differ from a plain program's by a relative error of at most 0.0057.
Values may be sent and summed in bfloat16 or wider, within the bound.
A program may use at most 128 MiB of HBM per device.

v0:
```python
import math
import jax
import jax.numpy as jnp
from jax import lax
from jax.sharding import PartitionSpec as P


def passed_along(value, axis, steps):
    count = lax.axis_size(axis)
    first, last = (max(0, -steps), min(count, count - steps))
    return lax.ppermute(value, axis, [(source, source + steps) for source in range(first, last)])


def depth_select(extent):
    inputs_z = jnp.arange(extent + 2)[None, :, None]
    outputs_z = jnp.arange(extent)[None, None, :]
    offsets_z = jnp.arange(3)[:, None, None]
    return (inputs_z == outputs_z + offsets_z).astype(jnp.float32)


def band_matrix(weights, extent):
    channels = weights.shape[1]
    cube = weights.astype(jnp.float32).reshape(3, 3, 3, channels, channels)
    banded = jnp.einsum(
        "dpq,abdio->abpiqo", depth_select(extent), cube, precision=lax.Precision.HIGHEST
    )
    return banded.reshape(3, 3, (extent + 2) * channels, extent * channels).astype(jnp.bfloat16)


def apply_band(padded, banded, extent):
    total = None
    for shift_x in range(3):
        for shift_y in range(3):
            window = padded[:, shift_x : shift_x + extent, shift_y : shift_y + extent, :]
            term = jnp.einsum(
                "nxyp,pq->nxyq",
                window,
                banded[shift_x, shift_y],
                preferred_element_type=jnp.float32,
            )
            total = term if total is None else total + term
    return total


def band_gradient(padded, gradient, extent, channels):
    select = depth_select(extent)
    pieces = []
    for shift_x in range(3):
        for shift_y in range(3):
            window = padded[:, shift_x : shift_x + extent, shift_y : shift_y + extent, :]
            outer = jnp.einsum(
                "nxyp,nxyq->pq", window, gradient, preferred_element_type=jnp.float32
            )
            outer = outer.reshape(extent + 2, channels, extent, channels)
            pieces.append(
                jnp.einsum("dpq,piqo->dio", select, outer, precision=lax.Precision.HIGHEST)
            )
    return jnp.stack(pieces).reshape(27, channels, channels)


def lift_bricks(latent_rows, up_weight, extent, channels):
    bricks_here = latent_rows.shape[0]
    blocks = latent_rows.reshape(bricks_here, 8, -1)
    cells = jnp.einsum("nci,io->nco", blocks, up_weight, preferred_element_type=jnp.float32)
    half = extent // 2
    shaped = cells.reshape(bricks_here, 2, 2, 2, half, half, half, channels)
    shaped = shaped.transpose(0, 1, 4, 2, 5, 3, 6, 7)
    return shaped.reshape(bricks_here, extent, extent, extent * channels).astype(jnp.bfloat16)


def face_planes(volume, channels):
    bricks_here, extent = (volume.shape[0], volume.shape[1])
    planes = [
        volume[:, 0],
        volume[:, extent - 1],
        volume[:, :, 0],
        volume[:, :, extent - 1],
        volume[:, :, :, 0:channels],
        volume[:, :, :, (extent - 1) * channels :],
    ]
    return jnp.stack([one_plane.reshape(bricks_here, -1) for one_plane in planes], axis=1)


def share_faces(stacked):
    from_left = passed_along(stacked, "space", 1)
    from_right = passed_along(stacked, "space", -1)
    return jnp.stack([from_left, stacked, from_right], axis=1)


def fill_padding(volume, face_pool, face_links, position, channels):
    bricks_here, extent = (volume.shape[0], volume.shape[1])
    neighbour = jnp.maximum(face_links, 0)
    source = jnp.clip(neighbour // bricks_here - position + 1, 0, 2)
    face_index = jnp.arange(6, dtype=jnp.int32)[None, :]
    row_index = (source * bricks_here + neighbour % bricks_here) * 6 + (face_index ^ 1)
    flattened = face_pool.reshape(3 * bricks_here * 6, -1)
    picked = jnp.take(flattened, row_index.reshape(-1), axis=0).reshape(bricks_here, 6, -1)
    picked = jnp.where((face_links >= 0)[:, :, None], picked, jnp.zeros((), picked.dtype))
    padded = jnp.pad(volume, ((0, 0), (1, 1), (1, 1), (channels, channels)))
    inside_range = slice(1, extent + 1)
    middle_range = slice(channels, (extent + 1) * channels)
    flat_face = (bricks_here, extent, extent * channels)
    depth_face = (bricks_here, extent, extent, channels)
    padded = padded.at[:, 0, inside_range, middle_range].set(picked[:, 0].reshape(flat_face))
    padded = padded.at[:, extent + 1, inside_range, middle_range].set(
        picked[:, 1].reshape(flat_face)
    )
    padded = padded.at[:, inside_range, 0, middle_range].set(picked[:, 2].reshape(flat_face))
    padded = padded.at[:, inside_range, extent + 1, middle_range].set(
        picked[:, 3].reshape(flat_face)
    )
    padded = padded.at[:, inside_range, inside_range, 0:channels].set(
        picked[:, 4].reshape(depth_face)
    )
    padded = padded.at[:, inside_range, inside_range, (extent + 1) * channels :].set(
        picked[:, 5].reshape(depth_face)
    )
    return padded


def body(coarse_latents, active_blocks, face_links, cotangent, up_weight, conv_one, conv_two):
    position = lax.axis_index("space")
    devices = lax.axis_size("space")
    bricks_here = face_links.shape[1]
    extent = cotangent.shape[2]
    channels = conv_one.shape[1]
    blocks_here = coarse_latents.shape[1]
    local_rows = coarse_latents[0]
    listed = active_blocks[0]
    mine = lax.dynamic_slice_in_dim(listed, position * bricks_here, bricks_here)
    owners = mine // blocks_here
    wanted = listed.reshape(devices, bricks_here)
    held = wanted // blocks_here == position
    local_index = jnp.clip(wanted - position * blocks_here, 0, blocks_here - 1)
    packed = jnp.where(
        held[:, :, None], jnp.take(local_rows, local_index, axis=0), jnp.zeros((), local_rows.dtype)
    )
    received = lax.all_to_all(packed, "space", split_axis=0, concat_axis=0, tiled=True)
    latent_rows = received[owners, jnp.arange(bricks_here)]
    lifted = lift_bricks(latent_rows, up_weight, extent, channels)
    links = face_links[0]
    upstream = cotangent[0]
    lifted_pool = share_faces(face_planes(lifted, channels)[None])[0]
    lifted_pad = fill_padding(lifted, lifted_pool, links, position, channels)
    band_one = band_matrix(conv_one, extent)
    band_two = band_matrix(conv_two, extent)
    band_back = band_matrix(jnp.flip(conv_two, axis=0).transpose(0, 2, 1), extent)
    pre = apply_band(lifted_pad, band_one, extent)
    hidden = jax.nn.silu(pre).astype(jnp.bfloat16)
    hidden_pool = share_faces(face_planes(hidden, channels)[None])[0]
    hidden_pad = fill_padding(hidden, hidden_pool, links, position, channels)
    fine = (lifted.astype(jnp.float32) + apply_band(hidden_pad, band_two, extent)).astype(
        jnp.bfloat16
    )
    scale = 1.0 / math.sqrt(lax.axis_size("dp") * devices * bricks_here * extent**3)
    second_local = band_gradient(hidden_pad, upstream, extent, channels) * scale
    upstream_pool = share_faces(face_planes(upstream, channels)[None])[0]
    upstream_pad = fill_padding(upstream, upstream_pool, links, position, channels)
    back = apply_band(upstream_pad, band_back, extent)
    sigmoid = jax.nn.sigmoid(pre)
    grad_pre = (back * sigmoid * (1.0 + pre * (1.0 - sigmoid))).astype(jnp.bfloat16)
    first_local = band_gradient(lifted_pad, grad_pre, extent, channels) * scale
    grad_one, grad_two = lax.psum((first_local, second_local), ("space", "dp"))
    return (fine[None], grad_one, grad_two)


def solution(mesh):
    return jax.shard_map(
        body,
        mesh=mesh,
        in_specs=(
            P("dp", "space", None),
            P("dp", None),
            P("dp", "space", None),
            P("dp", "space", None, None, None),
            P(),
            P(),
            P(),
        ),
        out_specs=(P("dp", "space", None, None, None), P(), P()),
        check_vma=False,
    )
```

profile of v0, /device:TPU:1, one launch (start us, length us, event | category | flops | bytes accessed | tf_op | source)
XLA Modules:
  0.0 758.2 jit_solution(1332796535409045901)
XLA Ops:
  13.7 5.0 collective-permute-start.4
  25.9 19.5 %all-to-all-start = ((bf16[64,2,512]{2,1,0:T(2,128)(2,1)}), bf16[64,2,512]{2,1,0:T(2,128)(2,1)S(1)}, u32[]{:S(2)}, u32[]{:S(2)}) async-start(bf16[64,2,512]{2,1,0:T(2,128)(2,1)} %broadcast_select_fusion.1), calls=%async_computation | async-start | bytes 262144 | tf_op jit(solution)/shard_map/all_to_all | solution.py:138
  45.5 5.6 convert_bitcast_fusion.2
  51.7 5.7 convert_bitcast_fusion
  57.4 2.0 all-to-all-done
  65.3 3.2 collective-permute-start
  68.5 1.7 collective-permute-start.1
  70.2 5.6 convert_bitcast_fusion.1
  75.8 10.3 %copy.127 = bf16[3,3,10,32,8,32]{5,4,3,2,1,0:T(8,128)(2,1)} copy(bf16[3,3,10,32,8,32]{5,2,3,1,0,4:T(8,128)(2,1)} %convert_bitcast_fusion.2) | data formatting | bytes 2949120 | tf_op jit(solution)/shard_map/convert_element_type | solution.py:27
  86.2 7.2 convert_element_type.66
  93.7 10.3 %copy.141 = bf16[3,3,10,32,8,32]{5,4,3,2,1,0:T(8,128)(2,1)} copy(bf16[3,3,10,32,8,32]{5,2,3,1,0,4:T(8,128)(2,1)} %convert_bitcast_fusion) | data formatting | bytes 2949120 | tf_op jit(solution)/shard_map/convert_element_type | solution.py:27
  103.9 8.3 %convert_element_type.74 = bf16[3,3,320,256]{3,2,1,0:T(8,128)(2,1)} reshape(bf16[3,3,10,32,8,32]{5,4,3,2,1,0:T(8,128)(2,1)} %copy.141) | data formatting | bytes 2949120 | tf_op jit(solution)/shard_map/convert_element_type | solution.py:27
  112.2 10.4 %copy.134 = bf16[3,3,10,32,8,32]{5,4,3,2,1,0:T(8,128)(2,1)} copy(bf16[3,3,10,32,8,32]{5,2,3,1,0,4:T(8,128)(2,1)} %convert_bitcast_fusion.1) | data formatting | bytes 2949120 | tf_op jit(solution)/shard_map/convert_element_type | solution.py:27
  122.6 7.2 convert_element_type.70
  132.4 1.6 reshape_squeeze.9
  134.0 2.2 gather_fusion.2
  142.1 3.0 scatter.60
  145.1 2.9 scatter.61
  148.0 4.0 scatter.64
  152.0 4.0 scatter.65
  156.0 2.9 scatter.66
  158.9 5.7 scatter.69
  170.3 4.0 collective-permute-start.2
  182.9 2.7 scatter.84
  185.6 2.7 scatter.85
  189.0 5.0 scatter.89
  215.4 2.7 scatter.74
  218.1 2.7 scatter.75
  221.5 5.4 scatter.79
  228.4 1.5 fusion.69
  231.5 2.2 fusion.72
  235.2 2.2 fusion.75
  239.0 2.2 fusion.78
  241.8 1.5 fusion.81
  244.0 1.7 fusion.84
  246.4 1.5 fusion.87
  248.6 1.5 fusion.90
  250.9 1.5 fusion.93
  254.7 1.5 fusion.66
  260.3 1.8 fusion.60
  263.4 1.5 fusion.57
  266.2 1.5 fusion.54
  269.1 1.5 fusion.51
  271.9 1.5 fusion.48
  274.7 2.2 fusion.45
  283.1 464.4 %all-reduce.6.cloned.1.call-done = (f32[27,32,32]{2,1,0:T(8,128)}, f32[27,32,32]{2,1,0:T(8,128)}) async-done(((f32[27,32,32]{2,1,0:T(8,128)}, f32[27,32,32]{2,1,0:T(8,128)}), (f32[27,32,32]{2,1,0:T(8,128)}, f32[27,32,32]{2,1,0:T(8,128)})) %all-reduce.6.cloned.1.call-update) | async-done | bytes 221200 | tf_op jit(solution)/shard_map/psum | solution.py:163
  747.5 1.8 copy.510
  749.3 1.8 copy.511
  (253 shorter events, 93.7 us)
Async XLA Ops:
  7.2 16.7 %copy-start = (bf16[1,64,512]{2,1,0:T(8,128)(2,1)S(1)}, bf16[1,64,512]{2,1,0:T(8,128)(2,1)}, u32[]{:S(2)}) copy-start(bf16[1,64,512]{2,1,0:T(8,128)(2,1)} %param.45) | copy-start | bytes 196612
  7.2 38.3 %copy-start.8 = (bf16[27,32,32]{2,1,0:T(8,128)(2,1)S(1)}, bf16[27,32,32]{2,1,0:T(8,128)(2,1)}, u32[]{:S(2)}) copy-start(bf16[27,32,32]{2,1,0:T(8,128)(2,1)} %param.50) | copy-start | bytes 165892
  13.7 162.2 %collective-permute-start.4 = (bf16[1,2,6,2048]{3,1,2,0:T(2,128)(2,1)}, bf16[1,2,6,2048]{3,1,2,0:T(2,128)(2,1)}, u32[]{:S(2)}, u32[]{:S(2)}) collective-permute-start(bf16[1,2,6,2048]{3,1,2,0:T(2,128)(2,1)} %bitcast.92), channel_id=1, source_target_pairs={{0,8},{8,16},{16,24},{24,32},{32,40},{40,48},{48,56},{56,64},{64,7... | collective-permute-start | bytes 147464 | tf_op jit(solution)/shard_map/ppermute | solution.py:11
  18.7 157.2 %collective-permute-start.5 = (bf16[1,2,6,2048]{3,1,2,0:T(2,128)(2,1)}, bf16[1,2,6,2048]{3,1,2,0:T(2,128)(2,1)}, u32[]{:S(2)}, u32[]{:S(2)}) collective-permute-start(bf16[1,2,6,2048]{3,1,2,0:T(2,128)(2,1)} %bitcast.92), channel_id=1, source_target_pairs={{8,0},{16,8},{24,16},{32,24},{40,32},{48,40},{56,48},{64,56},{72,6... | collective-permute-start | bytes 147464 | tf_op jit(solution)/shard_map/ppermute | solution.py:11
  21.3 116.5 %copy-start.16 = (pred[2,6]{1,0:T(4,128)(4,1)}, pred[2,6]{1,0:T(4,128)(4,1)S(1)}, u32[]{:S(2)}) copy-start(pred[2,6]{1,0:T(4,128)(4,1)S(1)} %get-tuple-element.285) | copy-start | bytes 40
  23.8 112.4 %copy-start.14 = (pred[12]{0:T(512)(128)(4,1)}, pred[12]{0:T(512)(128)(4,1)S(1)}, u32[]{:S(2)}) copy-start(pred[12]{0:T(512)(128)(4,1)S(1)} %get-tuple-element.242) | copy-start | bytes 40
  25.9 33.5 %all-to-all-start = ((bf16[64,2,512]{2,1,0:T(2,128)(2,1)}), bf16[64,2,512]{2,1,0:T(2,128)(2,1)S(1)}, u32[]{:S(2)}, u32[]{:S(2)}) async-start(bf16[64,2,512]{2,1,0:T(2,128)(2,1)} %broadcast_select_fusion.1), calls=%async_computation | async-start | bytes 262144 | tf_op jit(solution)/shard_map/all_to_all | solution.py:138
  45.4 702.1 %all-reduce.6.cloned.1.call-start = ((), (), s32[]{:S(2)}) async-start(), calls=%async_computation.1 | async-start | bytes 1769472 | tf_op jit(solution)/shard_map/psum | solution.py:163
  45.5 5.6 copy-start.18
  45.5 5.7 copy-start.9
  45.5 6.0 copy-start.6
  61.2 68.5 %copy-start.4 = (bf16[2,8,8,256]{3,2,1,0:T(8,128)(2,1)}, bf16[2,8,8,256]{3,2,1,0:T(8,128)(2,1)S(1)}, u32[]{:S(2)}) copy-start(bf16[2,8,8,256]{3,2,1,0:T(8,128)(2,1)S(1)} %convert_element_type.62) | copy-start | bytes 196612
  65.3 65.3 %collective-permute-start = (bf16[1,2,6,2048]{3,1,2,0:T(2,128)(2,1)}, bf16[1,2,6,2048]{3,1,2,0:T(2,128)(2,1)}, u32[]{:S(2)}, u32[]{:S(2)}) collective-permute-start(bf16[1,2,6,2048]{3,1,2,0:T(2,128)(2,1)} %bitcast.10), channel_id=1, source_target_pairs={{0,8},{8,16},{16,24},{24,32},{32,40},{40,48},{48,56},{56,64},{64,7... | collective-permute-start | bytes 147464 | tf_op jit(solution)/shard_map/ppermute | solution.py:11
  68.5 62.1 %collective-permute-start.1 = (bf16[1,2,6,2048]{3,1,2,0:T(2,128)(2,1)}, bf16[1,2,6,2048]{3,1,2,0:T(2,128)(2,1)}, u32[]{:S(2)}, u32[]{:S(2)}) collective-permute-start(bf16[1,2,6,2048]{3,1,2,0:T(2,128)(2,1)} %bitcast.10), channel_id=1, source_target_pairs={{8,0},{16,8},{24,16},{32,24},{40,32},{48,40},{56,48},{64,56},{72,6... | collective-permute-start | bytes 147464 | tf_op jit(solution)/shard_map/ppermute | solution.py:11
  86.2 7.2 copy-start.7
  164.6 3.4 copy-start.2
  170.3 7.5 collective-permute-start.2
  174.3 4.8 collective-permute-start.3
  177.0 3.1 copy-start.15
  177.1 3.2 copy-start.17
  196.2 6.7 copy-start.19
  199.6 4.5 copy-start.3
  250.8 1.6 copy-start.10
  250.9 1.6 copy-start.11
  250.9 1.6 copy-start.12
  278.2 1.6 copy-start.13
  281.5 0.8 copy-start.5
  282.2 468.9 %copy-start.1 = (bf16[1,64,512]{2,1,0:T(8,128)(2,1)S(1)}, bf16[1,64,512]{2,1,0:T(8,128)(2,1)}, u32[]{:S(2)}) copy-start(bf16[1,64,512]{2,1,0:T(8,128)(2,1)} %param.45) | copy-start | bytes 196612
Sparse Core Ops, SparseCore 0:
  282.4 465.0 all-reduce.5
where the time goes:
time: 766 us; the launch traced here: 758 us
  waiting for transfers between devices  468 us (61%)
  local copies, waits for them, and re-layouts  151 us (20%)
  matrix products  77.9 us (10%)
  starting transfers between devices  36.3 us (5%)
  between operations  15.5 us (2%)
  other arithmetic  9.85 us (1%)
    psum x1, waiting for transfers between devices, body(): grad_one, grad_two = lax.psum((first_local, second_local), ('space', 'dp'))  464 us
    convert_element_type x6, local copies, waits for them, and re-layouts, band_matrix(): banded.reshape(3, 3, (extent + 2) * channels, extent * channels)  53.6 us
    dot_general x18, matrix products, band_gradient(): jnp.einsum('dpq,piqo->dio', select, outer, precision=lax.Precision.HIGHEST)  30.7 us
    all_to_all x1, starting transfers between devices, body(): lax.all_to_all(packed, 'space', split_axis=0, concat_axis=0, tiled=True)  19.5 us
    dot_general x27, matrix products, apply_band(): jnp.einsum('nxyp,pq->nxyq', window, banded[shift_x, shift_y], preferred_e...  17.4 us
    dot_general x3, matrix products, band_matrix(): jnp.einsum('dpq,abdio->abpiqo', depth_select(extent), cube, precision=lax...  16.8 us
    ppermute x6, starting transfers between devices, passed_along(): lax.ppermute(value, axis, [(source, source + steps) for source in range(f...  16.7 us
    scatter x3, local copies, waits for them, and re-layouts, fill_padding(): padded.at[:, inside_range, inside_range, (extent + 1) * channels:]  16.1 us
  transfers between devices with their start and end apart: 8, of which 3 were waited for; matrix products, arithmetic and copies ran while one was open for 17% of the time, Pallas kernels for 0%

commit v1 on v0

--- a/solution.py
+++ b/solution.py
@@ -160,7 +160,15 @@
     sigmoid = jax.nn.sigmoid(pre)
     grad_pre = (back * sigmoid * (1.0 + pre * (1.0 - sigmoid))).astype(jnp.bfloat16)
     first_local = band_gradient(lifted_pad, grad_pre, extent, channels) * scale
-    grad_one, grad_two = lax.psum((first_local, second_local), ("space", "dp"))
+
+    def pieces_all_clear(page):
+        dev_axis = "space"
+        peer_axis = "dp"
+        for idx in (peer_axis, dev_axis):
+            page = lax.psum(page, idx)
+        return page
+
+    grad_one, grad_two = pieces_all_clear((first_local, second_local))
     return (fine[None], grad_one, grad_two)
 
 

time: 766 us -> 654 us (0.85)
  the two profiles are of different devices: /device:TPU:1 before, /device:TPU:2 now
where the time goes in v1:
time: 654 us; the launch traced here: 646 us
  waiting for transfers between devices  355 us (54%)
  local copies, waits for them, and re-layouts  151 us (23%)
  matrix products  77.9 us (12%)
  starting transfers between devices  37.1 us (6%)
  between operations  15.6 us (2%)
  other arithmetic  9.85 us (2%)
    psum x2, waiting for transfers between devices, pieces_all_clear(): page = lax.psum(page, idx)  349 us
    convert_element_type x6, local copies, waits for them, and re-layouts, band_matrix(): banded.reshape(3, 3, (extent + 2) * channels, extent * channels)  53.6 us
    dot_general x18, matrix products, band_gradient(): jnp.einsum('dpq,piqo->dio', select, outer, precision=lax.Precision.HIGHEST)  30.7 us
    all_to_all x1, starting transfers between devices, body(): lax.all_to_all(packed, 'space', split_axis=0, concat_axis=0, tiled=True)  20.1 us
    dot_general x27, matrix products, apply_band(): jnp.einsum('nxyp,pq->nxyq', window, banded[shift_x, shift_y], preferred_e...  17.4 us
    ppermute x6, starting transfers between devices, passed_along(): lax.ppermute(value, axis, [(source, source + steps) for source in range(f...  16.9 us
    dot_general x3, matrix products, band_matrix(): jnp.einsum('dpq,abdio->abpiqo', depth_select(extent), cube, precision=lax...  16.8 us
    scatter x3, local copies, waits for them, and re-layouts, fill_padding(): padded.at[:, inside_range, inside_range, (extent + 1) * channels:]  16.1 us
  transfers between devices with their start and end apart: 9, of which 4 were waited for; matrix products, arithmetic and copies ran while one was open for 20% of the time, Pallas kernels for 0%

profile of v1, /device:TPU:2, one launch (start us, length us, event | category | flops | bytes accessed | tf_op | source)
XLA Modules:
  0.0 646.3 jit_solution(12702054438642683129)
XLA Ops:
  13.7 4.4 collective-permute-start.4
  25.4 20.1 %all-to-all-start = ((bf16[64,2,512]{2,1,0:T(2,128)(2,1)}), bf16[64,2,512]{2,1,0:T(2,128)(2,1)S(1)}, u32[]{:S(2)}, u32[]{:S(2)}) async-start(bf16[64,2,512]{2,1,0:T(2,128)(2,1)} %broadcast_select_fusion.1), calls=%async_computation | async-start | bytes 262144 | tf_op jit(solution)/shard_map/all_to_all | solution.py:138
  45.5 5.6 convert_bitcast_fusion.2
  51.7 5.7 convert_bitcast_fusion
  57.4 4.0 all-to-all-done
  67.2 3.4 collective-permute-start
  70.7 1.7 collective-permute-start.1
  72.4 5.6 convert_bitcast_fusion.1
  78.0 10.3 %copy.127 = bf16[3,3,10,32,8,32]{5,4,3,2,1,0:T(8,128)(2,1)} copy(bf16[3,3,10,32,8,32]{5,2,3,1,0,4:T(8,128)(2,1)} %convert_bitcast_fusion.2) | data formatting | bytes 2949120 | tf_op jit(solution)/shard_map/convert_element_type | solution.py:27
  88.4 7.2 %convert_element_type.66 = bf16[3,3,320,256]{3,2,1,0:T(8,128)(2,1)S(1)} reshape(bf16[3,3,10,32,8,32]{5,4,3,2,1,0:T(8,128)(2,1)} %copy.127) | data formatting | bytes 2949120 | tf_op jit(solution)/shard_map/convert_element_type | solution.py:27
  95.9 10.3 %copy.141 = bf16[3,3,10,32,8,32]{5,4,3,2,1,0:T(8,128)(2,1)} copy(bf16[3,3,10,32,8,32]{5,2,3,1,0,4:T(8,128)(2,1)} %convert_bitcast_fusion) | data formatting | bytes 2949120 | tf_op jit(solution)/shard_map/convert_element_type | solution.py:27
  106.1 8.3 %convert_element_type.74 = bf16[3,3,320,256]{3,2,1,0:T(8,128)(2,1)} reshape(bf16[3,3,10,32,8,32]{5,4,3,2,1,0:T(8,128)(2,1)} %copy.141) | data formatting | bytes 2949120 | tf_op jit(solution)/shard_map/convert_element_type | solution.py:27
  114.4 10.4 %copy.134 = bf16[3,3,10,32,8,32]{5,4,3,2,1,0:T(8,128)(2,1)} copy(bf16[3,3,10,32,8,32]{5,2,3,1,0,4:T(8,128)(2,1)} %convert_bitcast_fusion.1) | data formatting | bytes 2949120 | tf_op jit(solution)/shard_map/convert_element_type | solution.py:27
  124.7 7.2 %convert_element_type.70 = bf16[3,3,320,256]{3,2,1,0:T(8,128)(2,1)S(1)} reshape(bf16[3,3,10,32,8,32]{5,4,3,2,1,0:T(8,128)(2,1)} %copy.134) | data formatting | bytes 2949120 | tf_op jit(solution)/shard_map/convert_element_type | solution.py:27
  134.6 1.6 reshape_squeeze.9
  136.2 2.2 gather_fusion.2
  144.3 3.0 scatter.60
  147.2 2.9 scatter.61
  150.2 4.0 scatter.64
  154.2 4.0 scatter.65
  158.1 2.9 scatter.66
  161.1 5.7 scatter.69
  172.5 4.5 collective-permute-start.2
  180.6 2.5 collective-permute-done.3
  186.7 2.7 scatter.84
  189.5 2.7 scatter.85
  192.9 5.0 scatter.89
  219.3 2.7 scatter.74
  222.0 2.7 scatter.75
  225.4 5.4 scatter.79
  232.3 1.5 fusion.69
  235.4 2.2 fusion.72
  239.1 2.2 fusion.75
  242.9 2.2 fusion.78
  245.7 1.5 fusion.81
  247.9 1.7 fusion.84
  250.3 1.5 fusion.87
  252.5 1.5 fusion.90
  254.8 1.5 fusion.93
  258.5 1.5 fusion.66
  261.4 1.5 fusion.63
  264.2 1.8 fusion.60
  267.3 1.5 fusion.57
  278.6 2.2 fusion.45
  286.0 73.5 %all-reduce.10.cloned.1.call-done = (f32[27,32,32]{2,1,0:T(8,128)}, f32[27,32,32]{2,1,0:T(8,128)}) async-done(((f32[27,32,32]{2,1,0:T(8,128)}, f32[27,32,32]{2,1,0:T(8,128)}), (f32[27,32,32]{2,1,0:T(8,128)}, f32[27,32,32]{2,1,0:T(8,128)})) %all-reduce.10.cloned.1.call-update) | async-done | bytes 221200 | tf_op jit(solution)/shard_map/psum | solution.py:168
  360.5 275.1 %all-reduce.8.cloned.1.call-done = (f32[27,32,32]{2,1,0:T(8,128)}, f32[27,32,32]{2,1,0:T(8,128)}) async-done(((f32[27,32,32]{2,1,0:T(8,128)}, f32[27,32,32]{2,1,0:T(8,128)}), (f32[27,32,32]{2,1,0:T(8,128)}, f32[27,32,32]{2,1,0:T(8,128)})) %all-reduce.8.cloned.1.call-update) | async-done | bytes 221200 | tf_op jit(solution)/shard_map/psum | solution.py:168
  635.6 1.8 copy.512
  637.4 1.8 copy.513
  (256 shorter events, 95.5 us)
Async XLA Ops:
  7.2 16.1 %copy-start = (bf16[1,64,512]{2,1,0:T(8,128)(2,1)S(1)}, bf16[1,64,512]{2,1,0:T(8,128)(2,1)}, u32[]{:S(2)}) copy-start(bf16[1,64,512]{2,1,0:T(8,128)(2,1)} %param.45) | copy-start | bytes 196612
  7.2 38.3 %copy-start.8 = (bf16[27,32,32]{2,1,0:T(8,128)(2,1)S(1)}, bf16[27,32,32]{2,1,0:T(8,128)(2,1)}, u32[]{:S(2)}) copy-start(bf16[27,32,32]{2,1,0:T(8,128)(2,1)} %param.50) | copy-start | bytes 165892
  13.7 164.9 %collective-permute-start.4 = (bf16[1,2,6,2048]{3,1,2,0:T(2,128)(2,1)}, bf16[1,2,6,2048]{3,1,2,0:T(2,128)(2,1)}, u32[]{:S(2)}, u32[]{:S(2)}) collective-permute-start(bf16[1,2,6,2048]{3,1,2,0:T(2,128)(2,1)} %bitcast.92), channel_id=1, source_target_pairs={{0,8},{8,16},{16,24},{24,32},{32,40},{40,48},{48,56},{56,64},{64,7... | collective-permute-start | bytes 147464 | tf_op jit(solution)/shard_map/ppermute | solution.py:11
  18.1 160.5 %collective-permute-start.5 = (bf16[1,2,6,2048]{3,1,2,0:T(2,128)(2,1)}, bf16[1,2,6,2048]{3,1,2,0:T(2,128)(2,1)}, u32[]{:S(2)}, u32[]{:S(2)}) collective-permute-start(bf16[1,2,6,2048]{3,1,2,0:T(2,128)(2,1)} %bitcast.92), channel_id=1, source_target_pairs={{8,0},{16,8},{24,16},{32,24},{40,32},{48,40},{56,48},{64,56},{72,6... | collective-permute-start | bytes 147464 | tf_op jit(solution)/shard_map/ppermute | solution.py:11
  20.8 119.2 %copy-start.16 = (pred[2,6]{1,0:T(4,128)(4,1)}, pred[2,6]{1,0:T(4,128)(4,1)S(1)}, u32[]{:S(2)}) copy-start(pred[2,6]{1,0:T(4,128)(4,1)S(1)} %get-tuple-element.287) | copy-start | bytes 40
  23.3 115.1 %copy-start.14 = (pred[12]{0:T(512)(128)(4,1)}, pred[12]{0:T(512)(128)(4,1)S(1)}, u32[]{:S(2)}) copy-start(pred[12]{0:T(512)(128)(4,1)S(1)} %get-tuple-element.244) | copy-start | bytes 40
  25.4 36.0 %all-to-all-start = ((bf16[64,2,512]{2,1,0:T(2,128)(2,1)}), bf16[64,2,512]{2,1,0:T(2,128)(2,1)S(1)}, u32[]{:S(2)}, u32[]{:S(2)}) async-start(bf16[64,2,512]{2,1,0:T(2,128)(2,1)} %broadcast_select_fusion.1), calls=%async_computation | async-start | bytes 262144 | tf_op jit(solution)/shard_map/all_to_all | solution.py:138
  45.4 314.0 %all-reduce.10.cloned.1.call-start = ((), (), s32[]{:S(2)}) async-start(), calls=%async_computation.2 | async-start | bytes 1769472 | tf_op jit(solution)/shard_map/psum | solution.py:168
  45.5 5.6 copy-start.18
  45.5 5.7 copy-start.9
  45.5 6.0 copy-start.6
  63.1 68.8 %copy-start.4 = (bf16[2,8,8,256]{3,2,1,0:T(8,128)(2,1)}, bf16[2,8,8,256]{3,2,1,0:T(8,128)(2,1)S(1)}, u32[]{:S(2)}) copy-start(bf16[2,8,8,256]{3,2,1,0:T(8,128)(2,1)S(1)} %convert_element_type.62) | copy-start | bytes 196612
  67.2 65.5 %collective-permute-start = (bf16[1,2,6,2048]{3,1,2,0:T(2,128)(2,1)}, bf16[1,2,6,2048]{3,1,2,0:T(2,128)(2,1)}, u32[]{:S(2)}, u32[]{:S(2)}) collective-permute-start(bf16[1,2,6,2048]{3,1,2,0:T(2,128)(2,1)} %bitcast.10), channel_id=1, source_target_pairs={{0,8},{8,16},{16,24},{24,32},{32,40},{40,48},{48,56},{56,64},{64,7... | collective-permute-start | bytes 147464 | tf_op jit(solution)/shard_map/ppermute | solution.py:11
  70.7 62.1 %collective-permute-start.1 = (bf16[1,2,6,2048]{3,1,2,0:T(2,128)(2,1)}, bf16[1,2,6,2048]{3,1,2,0:T(2,128)(2,1)}, u32[]{:S(2)}, u32[]{:S(2)}) collective-permute-start(bf16[1,2,6,2048]{3,1,2,0:T(2,128)(2,1)} %bitcast.10), channel_id=1, source_target_pairs={{8,0},{16,8},{24,16},{32,24},{40,32},{48,40},{56,48},{64,56},{72,6... | collective-permute-start | bytes 147464 | tf_op jit(solution)/shard_map/ppermute | solution.py:11
  88.4 7.2 %copy-start.7 = (bf16[1,2,8,8,256]{4,3,2,1,0:T(8,128)(2,1)S(1)}, bf16[1,2,8,8,256]{4,3,2,1,0:T(8,128)(2,1)}, u32[]{:S(2)}) copy-start(bf16[1,2,8,8,256]{4,3,2,1,0:T(8,128)(2,1)} %param.48) | copy-start | bytes 196612
  166.8 3.4 copy-start.2
  172.5 8.0 %collective-permute-start.2 = (bf16[1,2,6,2048]{3,1,2,0:T(2,128)(2,1)S(1)}, bf16[1,2,6,2048]{3,1,2,0:T(2,128)(2,1)S(1)}, u32[]{:S(2)}, u32[]{:S(2)}) collective-permute-start(bf16[1,2,6,2048]{3,1,2,0:T(2,128)(2,1)S(1)} %bitcast.663), channel_id=1, source_target_pairs={{0,8},{8,16},{16,24},{24,32},{32,40},{40,48},{48,56},{56,64},{64,7... | collective-permute-start | bytes 147464 | tf_op jit(solution)/shard_map/ppermute | solution.py:11
  177.1 6.0 collective-permute-start.3
  179.8 4.3 copy-start.15
  179.8 4.3 copy-start.17
  200.1 6.7 %copy-start.19 = (f32[2,8,8,256]{3,2,1,0:T(8,128)S(1)}, f32[2,8,8,256]{3,2,1,0:T(8,128)}, u32[]{:S(2)}) copy-start(f32[2,8,8,256]{3,2,1,0:T(8,128)} %get-tuple-element.296) | copy-start | bytes 393220
  203.5 4.5 copy-start.3
  254.7 1.6 copy-start.10
  254.7 1.6 copy-start.11
  254.8 1.6 copy-start.12
  282.1 1.6 copy-start.13
  285.7 74.0 %copy-start.5 = (bf16[2,8,8,256]{3,2,1,0:T(8,128)(2,1)S(1)}, bf16[2,8,8,256]{3,2,1,0:T(8,128)(2,1)}, u32[]{:S(2)}) copy-start(bf16[2,8,8,256]{3,2,1,0:T(8,128)(2,1)} %copy-done.4) | copy-start | bytes 196612
  285.8 349.8 %all-reduce.8.cloned.1.call-start = ((), (), s32[]{:S(2)}) async-start(), calls=%async_computation.1 | async-start | bytes 1769472 | tf_op jit(solution)/shard_map/psum | solution.py:168
  359.5 279.7 %copy-start.1 = (bf16[1,64,512]{2,1,0:T(8,128)(2,1)S(1)}, bf16[1,64,512]{2,1,0:T(8,128)(2,1)}, u32[]{:S(2)}) copy-start(bf16[1,64,512]{2,1,0:T(8,128)(2,1)} %param.45) | copy-start | bytes 196612
Sparse Core Ops, SparseCore 0:
  285.9 73.5 all-reduce.9
  363.2 272.2 all-reduce.7
